TPU v7x, 128 devices: a whole 4x4x4 slice. The times are simulated.
128 devices in a mesh: gx: 16 (over y, z), gy: 8 (over x, core).
Axes of the slice: x: 4, y: 4, z: 4, core: 2. Of those that a mesh axis runs over, the one named last changes fastest.
Arguments:
- level_cotangent: float32 [256, 128, 128], P('gx', 'gy'), may hold values from -6 to 6
- velocity_cotangent: float32 [3, 256, 128, 128], P(None, 'gx', 'gy'), may hold values from -6 to 6
- fraction: float32 [2, 3, 256, 128, 128], P(None, None, 'gx', 'gy'), may hold values from 0 to 1
- shift_x: int32 [16, 8, 2], P('gx', 'gy'), may hold values from -2 to 2
- shift_y: int32 [16, 8, 2], P('gx', 'gy'), may hold values from -1 to 1
- region_labels: int32 [256, 128, 128], P('gx', 'gy'), may hold values 0 or 1
- phase_rates: float32 [2], replicated, may hold values from 0.04 to 0.16
Outputs:
- level_gradient: float32 [256, 128, 128], P('gx', 'gy')
- velocity_gradient: float32 [3, 256, 128, 128], P(None, 'gx', 'gy')
All inputs are finite; a program needn't handle non-finite values. No bound on the sum of `region_labels` on one device may be relied on, other than what follows from the above.
Results may differ from a plain program's by a relative error of at most 0.0001.
Values sent between devices are 32-bit elements; how exact they have to be, the bound alone decides.
A program may use at most 128 MiB of HBM per device.

v0:
```python
import jax
import jax.numpy as jnp
from jax import lax
from jax.sharding import PartitionSpec as P

STEPS = 2


BUOYANCY = 0.8


def shifted(value, axis, steps):
    count = lax.axis_size(axis)
    pairs = [(source, (source + steps) % count) for source in range(count)]
    return lax.ppermute(value, axis, pairs)


def extended(cells, sides, width):
    for axis, dim in sides:
        count = lax.axis_size(axis)
        head = lax.slice_in_dim(cells, 0, width, axis=dim)
        tail = lax.slice_in_dim(cells, cells.shape[dim] - width, cells.shape[dim], axis=dim)
        cells = jnp.concatenate(
            [
                lax.ppermute(tail, axis, [(i, (i + 1) % count) for i in range(count)]),
                cells,
                lax.ppermute(head, axis, [((i + 1) % count, i) for i in range(count)]),
            ],
            axis=dim,
        )
    return cells


def cubic_weights(position):
    squared = position * position
    cubed = squared * position
    return (
        (2.0 * squared - cubed - position) * 0.5,
        (3.0 * cubed - 5.0 * squared + 2.0) * 0.5,
        (4.0 * squared - 3.0 * cubed + position) * 0.5,
        (cubed - squared) * 0.5,
    )


def sweep(padded, rate_padded):
    middle = padded[:, 1:-1, 1:-1]
    rate_middle = rate_padded[1:-1, 1:-1]
    summed = middle
    sides = (
        (padded[:, 2:, 1:-1], rate_padded[2:, 1:-1]),
        (padded[:, :-2, 1:-1], rate_padded[:-2, 1:-1]),
        (padded[:, 1:-1, 2:], rate_padded[1:-1, 2:]),
        (padded[:, 1:-1, :-2], rate_padded[1:-1, :-2]),
    )
    for neighbour, neighbour_rate in sides:
        summed = summed + 0.5 * (rate_middle + neighbour_rate) * (neighbour - middle)
    for distance in (1, -1):
        summed = summed + 0.5 * (rate_middle + jnp.roll(rate_middle, distance, -1)) * (
            jnp.roll(middle, distance, -1) - middle
        )
    return summed


def spread_back(stacked, fractions):
    cells_x = stacked.shape[1]
    cells_y = stacked.shape[2]
    weights_x = cubic_weights(fractions[0])
    weights_y = cubic_weights(fractions[1])
    weights_z = cubic_weights(fractions[2])
    patches = jnp.zeros((4, cells_x + 3, cells_y + 3, stacked.shape[3]), jnp.float32)
    for off_x in range(4):
        for off_y in range(4):
            weighted = stacked * (weights_x[off_x] * weights_y[off_y])
            column = jnp.zeros_like(weighted)
            for off_z in range(4):
                column = column + jnp.roll(weighted * weights_z[off_z], off_z - 1, -1)
            patches = patches + jnp.pad(
                column, ((0, 0), (off_x, 3 - off_x), (off_y, 3 - off_y), (0, 0))
            )
    return patches


def route(patches, own_x, own_y):
    slot_stack = jnp.stack([jnp.where(own_y == move_y, patches, 0.0) for move_y in (-1, 0, 1)])
    arrived_slots = jnp.where(own_x == 0, slot_stack, 0.0)
    for move_x in (-2, -1, 1, 2):
        masked_part = jnp.where(own_x == move_x, slot_stack, 0.0)
        arrived_slots = arrived_slots + shifted(masked_part, "gx", move_x)
    received = arrived_slots[1]
    for move_y in (-1, 1):
        received = received + shifted(arrived_slots[move_y + 1], "gy", move_y)
    return received


def fold_rims(received):
    cells_x = received.shape[1] - 3
    inner = received[:, 1 : cells_x + 1]
    for distance, start_row, rim_rows in (
        (-1, cells_x - 1, received[:, 0:1]),
        (1, 0, received[:, cells_x + 1 : cells_x + 3]),
    ):
        arrived = shifted(rim_rows, "gx", distance)
        inner = inner + jnp.pad(
            arrived, ((0, 0), (start_row, cells_x - start_row - arrived.shape[1]), (0, 0), (0, 0))
        )
    cells_y = inner.shape[2] - 3
    folded = inner[:, :, 1 : cells_y + 1]
    for distance, start_row, rim_rows in (
        (-1, cells_y - 1, inner[:, :, 0:1]),
        (1, 0, inner[:, :, cells_y + 1 : cells_y + 3]),
    ):
        arrived = shifted(rim_rows, "gy", distance)
        folded = folded + jnp.pad(
            arrived, ((0, 0), (0, 0), (start_row, cells_y - start_row - arrived.shape[2]), (0, 0))
        )
    return folded


def on_device(
    level_cotangent, velocity_cotangent, fraction, shift_x, shift_y, region_labels, phase_rates
):
    cell_rate = jnp.where(region_labels == 1, phase_rates[1], phase_rates[0])
    rate_deep = extended(cell_rate, (("gx", 0), ("gy", 1)), 2)
    rate_near = rate_deep[1:-1, 1:-1]
    level_now = level_cotangent
    velocity_now = velocity_cotangent
    for step_index in range(STEPS - 1, -1, -1):
        padded = extended(velocity_now, (("gx", 1), ("gy", 2)), 2)
        diffused = sweep(sweep(padded, rate_deep), rate_near)
        level_part = level_now + BUOYANCY * diffused[2]
        stacked = jnp.concatenate([level_part[None], diffused], 0)
        patches = spread_back(stacked, fraction[step_index])
        received = route(patches, shift_x[0, 0, step_index], shift_y[0, 0, step_index])
        moved = fold_rims(received)
        level_now = moved[0]
        velocity_now = moved[1:]
    return (level_now, velocity_now)


def solution(mesh):
    in_specs = (
        P("gx", "gy", None),
        P(None, "gx", "gy", None),
        P(None, None, "gx", "gy", None),
        P("gx", "gy", None),
        P("gx", "gy", None),
        P("gx", "gy", None),
        P(),
    )
    out_specs = (P("gx", "gy", None), P(None, "gx", "gy", None))
    return jax.shard_map(
        on_device, mesh=mesh, in_specs=in_specs, out_specs=out_specs, check_vma=False
    )
```

profile of v0, /device:TPU:0, one launch (start us, length us, event | category | flops | bytes accessed | tf_op | source)
XLA Modules:
  0.0 667.7 jit_solution(389521660469557092)
XLA Ops:
  6.2 4.7 collective-permute-start.5
  11.9 5.4 collective-permute-start.1
  40.7 4.8 multiply_multiply_fusion.94
  97.5 3.5 fusion.59
  101.1 3.6 fusion.63
  104.8 3.2 fusion.67
  125.1 5.6 collective-permute-start.8
  130.7 3.2 collective-permute-start.9
  134.5 89.2 %collective-permute-done.10 = f32[3,4,19,19,128]{4,1,3,2,0:T(4,128)S(1)} collective-permute-done((f32[3,4,19,19,128]{4,1,3,2,0:T(4,128)S(1)}, f32[3,4,19,19,128]{4,1,3,2,0:T(4,128)S(1)}, u32[]{:S(2)}, u32[]{:S(2)}) %collective-permute-start.10) | collective-permute-done | bytes 2218016 | tf_op jit(solution)/shard_map/ppermute | solution.py:15
  223.7 43.8 %collective-permute-done.11 = f32[3,4,19,19,128]{4,1,3,2,0:T(4,128)S(1)} collective-permute-done((f32[3,4,19,19,128]{4,1,3,2,0:T(4,128)S(1)}, f32[3,4,19,19,128]{4,1,3,2,0:T(4,128)S(1)}, u32[]{:S(2)}, u32[]{:S(2)}) %collective-permute-start.11) | collective-permute-done | bytes 2218016 | tf_op jit(solution)/shard_map/ppermute | solution.py:15
  267.5 7.0 %collective-permute-done.8 = f32[3,4,19,19,128]{4,1,3,2,0:T(4,128)S(1)} collective-permute-done((f32[3,4,19,19,128]{4,1,3,2,0:T(4,128)S(1)}, f32[3,4,19,19,128]{4,1,3,2,0:T(4,128)S(1)}, u32[]{:S(2)}, u32[]{:S(2)}) %collective-permute-start.8) | collective-permute-done | bytes 2218016 | tf_op jit(solution)/shard_map/ppermute | solution.py:15
  274.5 39.7 %collective-permute-done.9 = f32[3,4,19,19,128]{4,1,3,2,0:T(4,128)S(1)} collective-permute-done((f32[3,4,19,19,128]{4,1,3,2,0:T(4,128)S(1)}, f32[3,4,19,19,128]{4,1,3,2,0:T(4,128)S(1)}, u32[]{:S(2)}, u32[]{:S(2)}) %collective-permute-start.9) | collective-permute-done | bytes 2218016 | tf_op jit(solution)/shard_map/ppermute | solution.py:15
  317.3 9.0 %collective-permute-done.12 = f32[4,19,19,128]{3,0,2,1:T(4,128)S(1)} collective-permute-done((f32[4,19,19,128]{3,0,2,1:T(4,128)S(1)}, f32[4,19,19,128]{3,0,2,1:T(4,128)S(1)}, u32[]{:S(2)}, u32[]{:S(2)}) %collective-permute-start.12) | collective-permute-done | bytes 739360 | tf_op jit(solution)/shard_map/ppermute | solution.py:15
  330.0 5.3 collective-permute-start.14
  342.9 5.3 collective-permute-start.19
  365.2 4.7 multiply_multiply_fusion.46
  418.6 3.5 fusion.93
  422.2 3.6 fusion.97
  425.8 3.5 fusion.101
  445.6 3.1 collective-permute-start.22
  454.8 138.5 %collective-permute-done.22 = f32[3,4,19,19,128]{4,1,3,2,0:T(4,128)S(1)} collective-permute-done((f32[3,4,19,19,128]{4,1,3,2,0:T(4,128)S(1)}, f32[3,4,19,19,128]{4,1,3,2,0:T(4,128)S(1)}, u32[]{:S(2)}, u32[]{:S(2)}) %collective-permute-start.22) | collective-permute-done | bytes 2218016 | tf_op jit(solution)/shard_map/ppermute | solution.py:15
  595.4 8.5 %collective-permute-done.26 = f32[4,19,19,128]{3,0,2,1:T(4,128)S(1)} collective-permute-done((f32[4,19,19,128]{3,0,2,1:T(4,128)S(1)}, f32[4,19,19,128]{3,0,2,1:T(4,128)S(1)}, u32[]{:S(2)}, u32[]{:S(2)}) %collective-permute-start.26) | collective-permute-done | bytes 739360 | tf_op jit(solution)/shard_map/ppermute | solution.py:15
  603.9 3.1 collective-permute-done.27
  609.8 48.4 %collective-permute-start.28 = (f32[4,1,19,128]{3,0,2,1:T(4,128)S(1)}, f32[4,1,19,128]{3,0,2,1:T(4,128)S(1)}, u32[]{:S(2)}, u32[]{:S(2)}) collective-permute-start(f32[4,1,19,128]{3,0,2,1:T(4,128)S(1)} %slice.1532), channel_id=1, source_target_pairs={{0,120},{8,0},{16,8},{24,16},{32,24},{40,32},{48,40},{56,48},{64,5... | collective-permute-start | bytes 116744 | tf_op jit(solution)/shard_map/ppermute | solution.py:15
  (385 shorter events, 204.3 us)
Async XLA Ops:
  4.2 15.9 %collective-permute-start.4 = (f32[2,16,128]{2,1,0:T(8,128)S(1)}, f32[2,16,128]{2,1,0:T(8,128)S(1)}, u32[]{:S(2)}, u32[]{:S(2)}) collective-permute-start(f32[2,16,128]{2,1,0:T(8,128)S(1)} %get-tuple-element.240), channel_id=1, source_target_pairs={{0,8},{8,16},{16,24},{24,32},{32,40},{40,48},{48,56},{56,64},{64,7... | collective-permute-start | bytes 49160 | tf_op jit(solution)/shard_map/ppermute | solution.py:25
  6.2 13.8 %collective-permute-start.5 = (f32[2,16,128]{2,1,0:T(8,128)S(1)}, f32[2,16,128]{2,1,0:T(8,128)S(1)}, u32[]{:S(2)}, u32[]{:S(2)}) collective-permute-start(f32[2,16,128]{2,1,0:T(8,128)S(1)} %get-tuple-element.241), channel_id=1, source_target_pairs={{8,0},{16,8},{24,16},{32,24},{40,32},{48,40},{56,48},{64,56},{72,6... | collective-permute-start | bytes 49160 | tf_op jit(solution)/shard_map/ppermute | solution.py:27
  11.7 17.1 %collective-permute-start = (f32[3,2,16,128]{3,0,2,1:T(4,128)S(1)}, f32[3,2,16,128]{3,0,2,1:T(4,128)S(1)}, u32[]{:S(2)}, u32[]{:S(2)}) collective-permute-start(f32[3,2,16,128]{3,0,2,1:T(4,128)S(1)} %copy.17), channel_id=1, source_target_pairs={{0,8},{8,16},{16,24},{24,32},{32,40},{40,48},{48,56},{56,64},{64,7... | collective-permute-start | bytes 147464 | tf_op jit(solution)/shard_map/ppermute | solution.py:25
  11.9 17.9 %collective-permute-start.1 = (f32[3,2,16,128]{3,0,2,1:T(4,128)S(1)}, f32[3,2,16,128]{3,0,2,1:T(4,128)S(1)}, u32[]{:S(2)}, u32[]{:S(2)}) collective-permute-start(f32[3,2,16,128]{3,0,2,1:T(4,128)S(1)} %copy.18), channel_id=1, source_target_pairs={{8,0},{16,8},{24,16},{32,24},{40,32},{48,40},{56,48},{64,56},{72,6... | collective-permute-start | bytes 147464 | tf_op jit(solution)/shard_map/ppermute | solution.py:27
  20.1 8.0 %collective-permute-start.6 = (f32[20,2,128]{2,1,0:T(2,128)S(1)}, f32[20,2,128]{2,1,0:T(2,128)S(1)}, u32[]{:S(2)}, u32[]{:S(2)}) collective-permute-start(f32[20,2,128]{2,1,0:T(2,128)S(1)} %get-tuple-element.234), channel_id=1, source_target_pairs={{0,1},{1,2},{2,3},{3,4},{4,5},{5,6},{6,7},{7,0},{8,9},{9,10},{10,1... | collective-permute-start | bytes 61448 | tf_op jit(solution)/shard_map/ppermute | solution.py:25
  20.1 8.0 %collective-permute-start.7 = (f32[20,2,128]{2,1,0:T(2,128)S(1)}, f32[20,2,128]{2,1,0:T(2,128)S(1)}, u32[]{:S(2)}, u32[]{:S(2)}) collective-permute-start(f32[20,2,128]{2,1,0:T(2,128)S(1)} %get-tuple-element.235), channel_id=1, source_target_pairs={{1,0},{2,1},{3,2},{4,3},{5,4},{6,5},{7,6},{0,7},{9,8},{10,9},{11,1... | collective-permute-start | bytes 61448 | tf_op jit(solution)/shard_map/ppermute | solution.py:27
  124.9 98.8 %collective-permute-start.10 = (f32[3,4,19,19,128]{4,1,3,2,0:T(4,128)S(1)}, f32[3,4,19,19,128]{4,1,3,2,0:T(4,128)S(1)}, u32[]{:S(2)}, u32[]{:S(2)}) collective-permute-start(f32[3,4,19,19,128]{4,1,3,2,0:T(4,128)S(1)} %get-tuple-element.24), channel_id=1, source_target_pairs={{0,8},{8,16},{16,24},{24,32},{32,40},{40,48},{48,56},{56,64},{64,7... | collective-permute-start | bytes 6653960 | tf_op jit(solution)/shard_map/ppermute | solution.py:15
  125.0 142.5 %collective-permute-start.11 = (f32[3,4,19,19,128]{4,1,3,2,0:T(4,128)S(1)}, f32[3,4,19,19,128]{4,1,3,2,0:T(4,128)S(1)}, u32[]{:S(2)}, u32[]{:S(2)}) collective-permute-start(f32[3,4,19,19,128]{4,1,3,2,0:T(4,128)S(1)} %get-tuple-element.25), channel_id=1, source_target_pairs={{0,16},{8,24},{16,32},{24,40},{32,48},{40,56},{48,64},{56,72},{64,... | collective-permute-start | bytes 6653960 | tf_op jit(solution)/shard_map/ppermute | solution.py:15
  125.1 149.4 %collective-permute-start.8 = (f32[3,4,19,19,128]{4,1,3,2,0:T(4,128)S(1)}, f32[3,4,19,19,128]{4,1,3,2,0:T(4,128)S(1)}, u32[]{:S(2)}, u32[]{:S(2)}) collective-permute-start(f32[3,4,19,19,128]{4,1,3,2,0:T(4,128)S(1)} %get-tuple-element.22), channel_id=1, source_target_pairs={{0,112},{8,120},{16,0},{24,8},{32,16},{40,24},{48,32},{56,40},{64,... | collective-permute-start | bytes 6653960 | tf_op jit(solution)/shard_map/ppermute | solution.py:15
  130.7 183.5 %collective-permute-start.9 = (f32[3,4,19,19,128]{4,1,3,2,0:T(4,128)S(1)}, f32[3,4,19,19,128]{4,1,3,2,0:T(4,128)S(1)}, u32[]{:S(2)}, u32[]{:S(2)}) collective-permute-start(f32[3,4,19,19,128]{4,1,3,2,0:T(4,128)S(1)} %get-tuple-element.23), channel_id=1, source_target_pairs={{0,120},{8,0},{16,8},{24,16},{32,24},{40,32},{48,40},{56,48},{64,5... | collective-permute-start | bytes 6653960 | tf_op jit(solution)/shard_map/ppermute | solution.py:15
  315.8 10.5 %collective-permute-start.12 = (f32[4,19,19,128]{3,0,2,1:T(4,128)S(1)}, f32[4,19,19,128]{3,0,2,1:T(4,128)S(1)}, u32[]{:S(2)}, u32[]{:S(2)}) collective-permute-start(f32[4,19,19,128]{3,0,2,1:T(4,128)S(1)} %get-tuple-element.20), channel_id=1, source_target_pairs={{0,7},{1,0},{2,1},{3,2},{4,3},{5,4},{6,5},{7,6},{8,15},{9,8},{10,9... | collective-permute-start | bytes 2217992 | tf_op jit(solution)/shard_map/ppermute | solution.py:15
  317.3 12.1 %collective-permute-start.13 = (f32[4,19,19,128]{3,0,2,1:T(4,128)S(1)}, f32[4,19,19,128]{3,0,2,1:T(4,128)S(1)}, u32[]{:S(2)}, u32[]{:S(2)}) collective-permute-start(f32[4,19,19,128]{3,0,2,1:T(4,128)S(1)} %get-tuple-element.21), channel_id=1, source_target_pairs={{0,1},{1,2},{2,3},{3,4},{4,5},{5,6},{6,7},{7,0},{8,9},{9,10},{10,1... | collective-permute-start | bytes 2217992 | tf_op jit(solution)/shard_map/ppermute | solution.py:15
  329.7 8.0 %collective-permute-start.15 = (f32[4,2,19,128]{3,0,2,1:T(4,128)S(1)}, f32[4,2,19,128]{3,0,2,1:T(4,128)S(1)}, u32[]{:S(2)}, u32[]{:S(2)}) collective-permute-start(f32[4,2,19,128]{3,0,2,1:T(4,128)S(1)} %slice.1407), channel_id=1, source_target_pairs={{0,8},{8,16},{16,24},{24,32},{32,40},{40,48},{48,56},{56,64},{64,7... | collective-permute-start | bytes 233480 | tf_op jit(solution)/shard_map/ppermute | solution.py:15
  342.8 7.7 %collective-permute-start.18 = (f32[3,2,16,128]{3,0,2,1:T(4,128)S(1)}, f32[3,2,16,128]{3,0,2,1:T(4,128)S(1)}, u32[]{:S(2)}, u32[]{:S(2)}) collective-permute-start(f32[3,2,16,128]{3,0,2,1:T(4,128)S(1)} %get-tuple-element.216), channel_id=1, source_target_pairs={{0,8},{8,16},{16,24},{24,32},{32,40},{40,48},{48,56},{56,64},{64,7... | collective-permute-start | bytes 147464 | tf_op jit(solution)/shard_map/ppermute | solution.py:25
  342.9 7.6 %collective-permute-start.19 = (f32[3,2,16,128]{3,0,2,1:T(4,128)S(1)}, f32[3,2,16,128]{3,0,2,1:T(4,128)S(1)}, u32[]{:S(2)}, u32[]{:S(2)}) collective-permute-start(f32[3,2,16,128]{3,0,2,1:T(4,128)S(1)} %get-tuple-element.217), channel_id=1, source_target_pairs={{8,0},{16,8},{24,16},{32,24},{40,32},{48,40},{56,48},{64,56},{72,6... | collective-permute-start | bytes 147464 | tf_op jit(solution)/shard_map/ppermute | solution.py:27
  350.5 7.4 %collective-permute-start.20 = (f32[3,20,2,128]{3,0,2,1:T(4,128)S(1)}, f32[3,20,2,128]{3,0,2,1:T(4,128)S(1)}, u32[]{:S(2)}, u32[]{:S(2)}) collective-permute-start(f32[3,20,2,128]{3,0,2,1:T(4,128)S(1)} %get-tuple-element.150), channel_id=1, source_target_pairs={{0,1},{1,2},{2,3},{3,4},{4,5},{5,6},{6,7},{7,0},{8,9},{9,10},{10,1... | collective-permute-start | bytes 184328 | tf_op jit(solution)/shard_map/ppermute | solution.py:25
  445.6 147.7 %collective-permute-start.22 = (f32[3,4,19,19,128]{4,1,3,2,0:T(4,128)S(1)}, f32[3,4,19,19,128]{4,1,3,2,0:T(4,128)S(1)}, u32[]{:S(2)}, u32[]{:S(2)}) collective-permute-start(f32[3,4,19,19,128]{4,1,3,2,0:T(4,128)S(1)} %get-tuple-element.16), channel_id=1, source_target_pairs={{0,112},{8,120},{16,0},{24,8},{32,16},{40,24},{48,32},{56,40},{64,... | collective-permute-start | bytes 6653960 | tf_op jit(solution)/shard_map/ppermute | solution.py:15
  448.7 144.6 %collective-permute-start.23 = (f32[3,4,19,19,128]{4,1,3,2,0:T(4,128)S(1)}, f32[3,4,19,19,128]{4,1,3,2,0:T(4,128)S(1)}, u32[]{:S(2)}, u32[]{:S(2)}) collective-permute-start(f32[3,4,19,19,128]{4,1,3,2,0:T(4,128)S(1)} %get-tuple-element.17), channel_id=1, source_target_pairs={{0,120},{8,0},{16,8},{24,16},{32,24},{40,32},{48,40},{56,48},{64,5... | collective-permute-start | bytes 6653960 | tf_op jit(solution)/shard_map/ppermute | solution.py:15
  451.1 142.3 %collective-permute-start.24 = (f32[3,4,19,19,128]{4,1,3,2,0:T(4,128)S(1)}, f32[3,4,19,19,128]{4,1,3,2,0:T(4,128)S(1)}, u32[]{:S(2)}, u32[]{:S(2)}) collective-permute-start(f32[3,4,19,19,128]{4,1,3,2,0:T(4,128)S(1)} %get-tuple-element.18), channel_id=1, source_target_pairs={{0,8},{8,16},{16,24},{24,32},{32,40},{40,48},{48,56},{56,64},{64,7... | collective-permute-start | bytes 6653960 | tf_op jit(solution)/shard_map/ppermute | solution.py:15
  451.9 141.5 %collective-permute-start.25 = (f32[3,4,19,19,128]{4,1,3,2,0:T(4,128)S(1)}, f32[3,4,19,19,128]{4,1,3,2,0:T(4,128)S(1)}, u32[]{:S(2)}, u32[]{:S(2)}) collective-permute-start(f32[3,4,19,19,128]{4,1,3,2,0:T(4,128)S(1)} %get-tuple-element.19), channel_id=1, source_target_pairs={{0,16},{8,24},{16,32},{24,40},{32,48},{40,56},{48,64},{56,72},{64,... | collective-permute-start | bytes 6653960 | tf_op jit(solution)/shard_map/ppermute | solution.py:15
  594.9 9.0 %collective-permute-start.26 = (f32[4,19,19,128]{3,0,2,1:T(4,128)S(1)}, f32[4,19,19,128]{3,0,2,1:T(4,128)S(1)}, u32[]{:S(2)}, u32[]{:S(2)}) collective-permute-start(f32[4,19,19,128]{3,0,2,1:T(4,128)S(1)} %get-tuple-element.14), channel_id=1, source_target_pairs={{0,7},{1,0},{2,1},{3,2},{4,3},{5,4},{6,5},{7,6},{8,15},{9,8},{10,9... | collective-permute-start | bytes 2217992 | tf_op jit(solution)/shard_map/ppermute | solution.py:15
  594.9 12.1 %collective-permute-start.27 = (f32[4,19,19,128]{3,0,2,1:T(4,128)S(1)}, f32[4,19,19,128]{3,0,2,1:T(4,128)S(1)}, u32[]{:S(2)}, u32[]{:S(2)}) collective-permute-start(f32[4,19,19,128]{3,0,2,1:T(4,128)S(1)} %get-tuple-element.15), channel_id=1, source_target_pairs={{0,1},{1,2},{2,3},{3,4},{4,5},{5,6},{6,7},{7,0},{8,9},{9,10},{10,1... | collective-permute-start | bytes 2217992 | tf_op jit(solution)/shard_map/ppermute | solution.py:15
  607.3 53.2 %collective-permute-start.29 = (f32[4,2,19,128]{3,0,2,1:T(4,128)S(1)}, f32[4,2,19,128]{3,0,2,1:T(4,128)S(1)}, u32[]{:S(2)}, u32[]{:S(2)}) collective-permute-start(f32[4,2,19,128]{3,0,2,1:T(4,128)S(1)} %slice.1533), channel_id=1, source_target_pairs={{0,8},{8,16},{16,24},{24,32},{32,40},{40,48},{48,56},{56,64},{64,7... | collective-permute-start | bytes 233480 | tf_op jit(solution)/shard_map/ppermute | solution.py:15
  609.8 50.1 %collective-permute-start.28 = (f32[4,1,19,128]{3,0,2,1:T(4,128)S(1)}, f32[4,1,19,128]{3,0,2,1:T(4,128)S(1)}, u32[]{:S(2)}, u32[]{:S(2)}) collective-permute-start(f32[4,1,19,128]{3,0,2,1:T(4,128)S(1)} %slice.1532), channel_id=1, source_target_pairs={{0,120},{8,0},{16,8},{24,16},{32,24},{40,32},{48,40},{56,48},{64,5... | collective-permute-start | bytes 116744 | tf_op jit(solution)/shard_map/ppermute | solution.py:15
  (85 other events, 285.9 us)
where the time goes:
time: 676 us; the launch traced here: 668 us
  waiting for transfers between devices  353 us (52%)
  starting transfers between devices  108 us (16%)
  local copies, waits for them, and re-layouts  107 us (16%)
  other arithmetic  85.6 us (13%)
  between operations  13.1 us (2%)
    ppermute x20, waiting for transfers between devices, shifted(): return lax.ppermute(value, axis, pairs)  350 us
    slice x96, local copies, waits for them, and re-layouts, spread_back(): column = column + jnp.roll(weighted * weights_z[off_z], off_z - 1, -1)  95.5 us
    ppermute x20, starting transfers between devices, shifted(): return lax.ppermute(value, axis, pairs)  82 us
    add x16, other arithmetic, spread_back(): column = column + jnp.roll(weighted * weights_z[off_z], off_z - 1, -1)  44.5 us
    ppermute x6, starting transfers between devices, extended(): lax.ppermute(head, axis, [((i + 1) % count, i) for i in range(count)])  24.2 us
    mul x6, other arithmetic, spread_back(): column = column + jnp.roll(weighted * weights_z[off_z], off_z - 1, -1)  15.5 us
  transfers between devices with their start and end apart: 32, of which 19 were waited for; matrix products, arithmetic and copies ran while one was open for 1% of the time, Pallas kernels for 0%

commit v1 on v0

v1 whole, which is shorter than its diff:
```python
import jax
import jax.numpy as jnp
from jax import lax
from jax.experimental import pallas as pl
from jax.experimental.pallas import tpu as pltpu
from jax.sharding import PartitionSpec as P

MESH = pl.DeviceIdType.MESH
BUOYANCY = 0.8
C = 16
Z = 128
ROW = (C, Z)
HALO = 24
PATCH = C + 3

PARTNERS = (
    [(d, 0) for d in (1, -1, 3, -3)]
    + [(0, d) for d in (1, -1, 2, -2)]
    + [(a, b) for a in (1, -1) for b in (1, -1)]
)


def cubic_weights(position):
    squared = position * position
    cubed = squared * position
    return (
        (2.0 * squared - cubed - position) * 0.5,
        (3.0 * cubed - 5.0 * squared + 2.0) * 0.5,
        (4.0 * squared - 3.0 * cubed + position) * 0.5,
        (cubed - squared) * 0.5,
    )


def rolled(value, shift, axis):
    shift = shift % value.shape[axis]
    return value if shift == 0 else pltpu.roll(value, shift, axis)


def make_kernel(count_x, count_y):
    def kernel(
        lev, vel, lab, frac_any, sx, sy, rates,
        out_l, out_v,
        frac, ext, mid, coef, dif, lvl, weight,
        to_up, to_down, to_rim, own, from_down, from_up, from_rim,
        edge_r, edge_l, tail_r, tail_l, got_tail_r, got_tail_l,
        got_r1, got_l1, next_r, next_l, got_r2, got_l2,
        send_sem, recv_sem, frac_sem,
    ):
        me_x = lax.axis_index("gx")
        me_y = lax.axis_index("gy")

        def partner(dx, dy):
            return (lax.rem(me_x + dx + count_x, count_x), lax.rem(me_y + dy + count_y, count_y))

        frac_copy = pltpu.make_async_copy(frac_any, frac, frac_sem)
        frac_copy.start()

        barrier = pltpu.get_barrier_semaphore()
        for dx, dy in PARTNERS:
            pl.semaphore_signal(barrier, inc=1, device_id=partner(dx, dy), device_id_type=MESH)

        started = []

        def send(src, dst, dx, dy):
            index = len(started)
            copy = pltpu.make_async_remote_copy(
                src_ref=src, dst_ref=dst, send_sem=send_sem.at[index], recv_sem=recv_sem.at[index],
                device_id=partner(dx, dy), device_id_type=MESH,
            )
            copy.start()
            started.append(copy)
            return copy

        for f in range(3):
            ext[0, f, 2 : C + 2, 0:C, :] = vel[f]
        ext[0, 3, 2 : C + 2, 0:C, :] = jnp.where(lab[...] == 1, rates[1], rates[0])
        pl.semaphore_wait(barrier, len(PARTNERS))

        def send_halo(step, fields):
            e = ext.at[step]
            lo, hi = C, C + 2
            f = pl.ds(0, fields)
            copies = [
                send(e.at[f, lo:hi, 0:C], e.at[f, 0:2, 0:C], 1, 0),
                send(e.at[f, 2:4, 0:C], e.at[f, hi : hi + 2, 0:C], -1, 0),
                send(e.at[f, 2:hi, C - 2 : C], e.at[f, 2:hi, HALO - 2 : HALO], 0, 1),
                send(e.at[f, 2:hi, 0:2], e.at[f, 2:hi, C : C + 2], 0, -1),
            ]
            for dx in (1, -1):
                for dy in (1, -1):
                    src_i, dst_i = (hi - 1, 1) if dx == 1 else (2, hi)
                    src_j, dst_j = (C - 1, HALO - 1) if dy == 1 else (0, C)
                    copies.append(
                        send(
                            e.at[f, src_i : src_i + 1, src_j : src_j + 1],
                            e.at[f, dst_i : dst_i + 1, dst_j : dst_j + 1],
                            dx, dy,
                        )
                    )
            return copies

        def coefficients():
            def body(i, carry):
                rate = ext[0, 3, i]
                k = [
                    0.5 * (rate + ext[0, 3, i + 1]),
                    0.5 * (rate + ext[0, 3, i - 1]),
                    0.5 * (rate + rolled(rate, -1, 0)),
                    0.5 * (rate + rolled(rate, 1, 0)),
                    0.5 * (rate + rolled(rate, -1, 1)),
                    0.5 * (rate + rolled(rate, 1, 1)),
                ]
                coef[0, i] = 1.0 - ((k[0] + k[1]) + (k[2] + k[3]) + (k[4] + k[5]))
                for n in range(6):
                    coef[n + 1, i] = k[n]
                return carry

            lax.fori_loop(1, C + 3, body, 0)

        def swept(src, f, i, height):
            v = src[f, i]
            low = slice(0, height)
            total = coef[0, i, low] * v[low]
            total += coef[1, i, low] * src[f, i + 1, low]
            total += coef[2, i, low] * src[f, i - 1, low]
            total += coef[3, i, low] * rolled(v, -1, 0)[low]
            total += coef[4, i, low] * rolled(v, 1, 0)[low]
            total += coef[5, i, low] * rolled(v[low], -1, 1)
            total += coef[6, i, low] * rolled(v[low], 1, 1)
            return total

        def diffuse(step):
            def first(i, carry):
                for f in range(3):
                    mid[f, i] = swept(ext.at[step], f, i, HALO)
                return carry

            lax.fori_loop(1, C + 3, first, 0)

            def second(i, carry):
                for f in range(3):
                    dif[f, i - 2] = swept(mid, f, i, C)
                return carry

            lax.fori_loop(2, C + 2, second, 0)

        def weights(step):
            def body(x, carry):
                for n, value in enumerate(cubic_weights(frac[step, 2, x])):
                    weight[n, x] = value
                for axis in range(2):
                    base = frac[step, axis, x]
                    for c in range(4):
                        for n, value in enumerate(cubic_weights(rolled(base, c - 1, 1))):
                            weight[4 + 16 * axis + 4 * c + n, x] = value
                return carry

            lax.fori_loop(0, C, body, 0)

        line = lax.broadcasted_iota(jnp.int32, ROW, 0)

        def spread(step, f, slot):
            row_y = jnp.full(ROW, sy[step], jnp.int32)
            up = jnp.where(row_y == 1, 1.0, 0.0)
            stay = jnp.where(row_y == 0, 1.0, 0.0)
            down = jnp.where(row_y == -1, 1.0, 0.0)
            high = line < C // 2
            stay_h = jnp.where(high, stay, 0.0)
            stay_l = jnp.where(high, 0.0, stay)
            rim_own = jnp.where(high, down, up)
            rim_far = jnp.where(high, up, down)

            def emit(r, main, rim):
                to_up[slot, r] = main * up + rim * stay_h
                to_down[slot, r] = main * down + rim * stay_l
                own[slot, r] = main * stay + rim * rim_own
                to_rim[slot, r] = rim * rim_far

            def body(x, carry):
                if f < 3:
                    g = dif[f, x]
                else:
                    g = lvl[x] + BUOYANCY * dif[2, x]
                sums = [[None] * 4 for _ in range(4)]
                for c in range(4):
                    gc = rolled(g * weight[c, x], c - 1, 1)
                    for b in range(4):
                        h = gc * weight[20 + 4 * c + b, x]
                        for a in range(4):
                            term = h * weight[4 + 4 * c + a, x]
                            sums[a][b] = term if c == 0 else sums[a][b] + term
                mains, rims = [], []
                for a in range(4):
                    below = rolled(sums[a][0], -1, 0)
                    above = rolled(sums[a][2], 1, 0)
                    above2 = rolled(sums[a][3], 2, 0)
                    mains.append(
                        sums[a][1]
                        + jnp.where(line == C - 1, 0.0, below)
                        + jnp.where(line == 0, 0.0, above)
                        + jnp.where(line < 2, 0.0, above2)
                    )
                    rims.append(
                        jnp.where(line == C - 1, below, 0.0)
                        + jnp.where(line == 0, above, 0.0)
                        + jnp.where(line < 2, above2, 0.0)
                    )
                m0, m1, m2, r0, r1, r2 = carry
                emit(x, m0 + mains[0], r0 + rims[0])
                return (m1 + mains[1], m2 + mains[2], mains[3], r1 + rims[1], r2 + rims[2], rims[3])

            zero = jnp.zeros(ROW, jnp.float32)
            m0, m1, m2, r0, r1, r2 = lax.fori_loop(0, C, body, (zero,) * 6)
            emit(C, m0, r0)
            emit(C + 1, m1, r1)
            emit(C + 2, m2, r2)
            meta = jnp.full(ROW, sx[step], jnp.int32).astype(jnp.float32)
            to_up[slot, PATCH] = meta
            to_down[slot, PATCH] = meta
            to_rim[slot, PATCH] = meta
            own[slot, PATCH] = meta
            return [
                send(to_up.at[slot], from_down.at[slot], 0, 1),
                send(to_down.at[slot], from_up.at[slot], 0, -1),
                send(to_rim.at[slot, :, 0:2], from_rim.at[slot, :, 0:2], 0, 2),
                send(to_rim.at[slot, :, C - 1 : C], from_rim.at[slot, :, C - 1 : C], 0, -2),
            ]

        sources = (own, from_down, from_up, from_rim)
        rim_lines = (line < 2) | (line == C - 1)

        def masks(slot, move):
            found = []
            for n, source in enumerate(sources):
                hit = source[slot, PATCH] == float(move)
                found.append(hit & rim_lines if n == 3 else hit)
            return found

        def gathered(slot, hits, r):
            total = None
            for hit, source in zip(hits, sources):
                part = jnp.where(hit, source[slot, r], 0.0)
                total = part if total is None else total + part
            return total

        def build(slot, move, store, load_extra=None):
            hits = masks(slot, move)
            before = masks(slot, move - 1) if move > -2 else None
            after = masks(slot, move + 1) if move < 2 else None

            def row(q, extra_sum):
                total = gathered(slot, hits, q + 1)
                if load_extra is not None:
                    total = total + load_extra(q)
                if extra_sum is not None:
                    total = total + extra_sum
                store(q, total)

            def body(q, carry):
                row(q, None)
                return carry

            first = 2 if before is not None else 0
            last = C - 1 if after is not None else C
            if before is not None:
                row(0, gathered(slot, before, C + 1))
                row(1, gathered(slot, before, C + 2))
            lax.fori_loop(first, last, body, 0)
            if after is not None:
                row(C - 1, gathered(slot, after, 0))

        def store_to(ref, slot):
            def store(q, value):
                ref[slot, q] = value

            return store

        def outer(slot):
            build(slot, 2, store_to(edge_r, slot))
            copies = [send(edge_r.at[slot], got_r1.at[slot], 1, 0)]
            build(slot, -2, store_to(edge_l, slot))
            copies.append(send(edge_l.at[slot], got_l1.at[slot], -1, 0))
            hits = masks(slot, 2)
            tail_r[slot, 0] = gathered(slot, hits, C + 1)
            tail_r[slot, 1] = gathered(slot, hits, C + 2)
            tail_l[slot, 0] = gathered(slot, masks(slot, -2), 0)
            copies.append(send(tail_r.at[slot], got_tail_r.at[slot], 3, 0))
            copies.append(send(tail_l.at[slot], got_tail_l.at[slot], -3, 0))
            return copies

        def inner(slot, copies):
            copies[0].wait_recv()
            build(slot, 1, store_to(next_r, slot), lambda q: got_r1[slot, q])
            right = send(next_r.at[slot], got_r2.at[slot], 1, 0)
            copies[1].wait_recv()
            build(slot, -1, store_to(next_l, slot), lambda q: got_l1[slot, q])
            left = send(next_l.at[slot], got_l2.at[slot], -1, 0)
            return [right, left, copies[2], copies[3]]

        def finish(slot, copies, load, store):
            for copy in copies:
                copy.wait_recv()
            build(slot, 0, store, lambda q: got_r2[slot, q] + got_l2[slot, q])
            store(0, load(0) + got_tail_r[slot, 0])
            store(1, load(1) + got_tail_r[slot, 1])
            store(C - 1, load(C - 1) + got_tail_l[slot, 0])

        def target(step, f):
            if step == 0 and f < 3:
                def store(q, value):
                    ext[1, f, q + 2, 0:C] = value

                def load(q):
                    return ext[1, f, q + 2, 0:C]
            elif step == 0:
                def store(q, value):
                    lvl[q] = value

                def load(q):
                    return lvl[q]
            elif f < 3:
                def store(q, value):
                    out_v[f, q] = value

                def load(q):
                    return out_v[f, q]
            else:
                def store(q, value):
                    out_l[q] = value

                def load(q):
                    return out_l[q]
            return load, store

        def wait_all(copies):
            for copy in copies:
                copy.wait_recv()

        halo = send_halo(0, 4)
        lvl[...] = lev[...]
        frac_copy.wait()
        weights(1)
        pending = None
        for step in range(2):
            when = 1 - step
            base = 4 * step
            wait_all(halo)
            if step == 0:
                coefficients()
            diffuse(step)
            chain = [None] * 4
            passed = [None] * 4
            passed[0] = spread(when, 0, base)
            passed[1] = spread(when, 1, base + 1)
            wait_all(passed[0])
            chain[0] = outer(base)
            passed[2] = spread(when, 2, base + 2)
            wait_all(passed[1])
            chain[1] = outer(base + 1)
            if step == 1:
                finish(base - 1, pending, *target(0, 3))
            passed[3] = spread(when, 3, base + 3)
            wait_all(passed[2])
            chain[2] = outer(base + 2)
            for f in range(3):
                chain[f] = inner(base + f, chain[f])
            wait_all(passed[3])
            chain[3] = outer(base + 3)
            if step == 0:
                weights(0)
            for f in range(3):
                finish(base + f, chain[f], *target(step, f))
            if step == 0:
                halo = send_halo(1, 3)
            pending = inner(base + 3, chain[3])
        finish(7, pending, *target(1, 3))
        for copy in started:
            copy.wait_send()

    return kernel


def solution(mesh):
    count_x, count_y = mesh.shape["gx"], mesh.shape["gy"]
    copies = 2 * (8 + 4 * 10)

    def on_device(level, velocity, fraction, shift_x, shift_y, labels, rates):
        vmem = pl.BlockSpec(memory_space=pltpu.VMEM)
        smem = pl.BlockSpec(memory_space=pltpu.SMEM)
        f32 = jnp.float32

        def rows(*lead):
            return pltpu.VMEM(lead + ROW, f32)

        return pl.pallas_call(
            make_kernel(count_x, count_y),
            name="adjoint",
            out_shape=(
                jax.ShapeDtypeStruct((C, C, Z), f32),
                jax.ShapeDtypeStruct((3, C, C, Z), f32),
            ),
            in_specs=[vmem, vmem, vmem, pl.BlockSpec(memory_space=pl.ANY), smem, smem, smem],
            out_specs=(vmem, vmem),
            scratch_shapes=[
                rows(2, 3, C),
                pltpu.VMEM((2, 4, C + 4, HALO, Z), f32),
                pltpu.VMEM((3, C + 4, HALO, Z), f32),
                pltpu.VMEM((7, C + 4, HALO, Z), f32),
                rows(3, C),
                rows(C),
                rows(36, C),
                rows(8, PATCH + 1), rows(8, PATCH + 1), rows(8, PATCH + 1), rows(8, PATCH + 1),
                rows(8, PATCH + 1), rows(8, PATCH + 1), rows(8, PATCH + 1),
                rows(8, C), rows(8, C), rows(8, 2), rows(8, 1), rows(8, 2), rows(8, 1),
                rows(8, C), rows(8, C), rows(8, C), rows(8, C), rows(8, C), rows(8, C),
                pltpu.SemaphoreType.DMA((copies,)),
                pltpu.SemaphoreType.DMA((copies,)),
                pltpu.SemaphoreType.DMA,
            ],
            compiler_params=pltpu.CompilerParams(
                collective_id=0, has_side_effects=True, vmem_limit_bytes=56 * 2**20
            ),
        )(level, velocity, labels, fraction, shift_x.reshape(2), shift_y.reshape(2), rates)

    field = P("gx", "gy", None)
    stack = P(None, "gx", "gy", None)
    return jax.shard_map(
        on_device,
        mesh=mesh,
        in_specs=(field, stack, P(None, None, "gx", "gy", None), field, field, field, P()),
        out_specs=(field, stack),
        check_vma=False,
    )
```

time: 676 us -> 99.2 us (0.15); the launches traced: 668 us -> 98.5 us
  waiting for transfers between devices: 353 us -> 0 us
  starting transfers between devices: 108 us -> 0 us
  local copies, waits for them, and re-layouts: 107 us -> 3.33 us
  Pallas kernels: 0 us -> 94.5 us
  other arithmetic: 85.6 us -> 0 us
  between operations: 13.1 us -> 0.64 us
    ppermute x32 -> x0, waiting for transfers between devices: 353 us -> none  [the longest x20 350 us: shifted(): return lax.ppermute(value, axis, pairs)]
    ppermute x32 -> x0, starting transfers between devices: 108 us -> none  [the longest x20 82 us: shifted(): return lax.ppermute(value, axis, pairs)]
    slice x127 -> x0, local copies, waits for them, and re-layouts: 104 us -> none  [the longest x96 95.5 us: spread_back(): column = column + jnp.roll(weighted * weights_z[off_z], off_z - 1, -1)]
    pallas_call x0 -> x1, Pallas kernels: none -> 94.5 us  [on_device(): pl.pallas_call(make_kernel(count_x, count_y), name='adjoint', out_shape=(...]
    add x30 -> x0, other arithmetic: 55.1 us -> none  [the longest x16 44.5 us: spread_back(): column = column + jnp.roll(weighted * weights_z[off_z], off_z - 1, -1)]
    mul x12 -> x0, other arithmetic: 19 us -> none  [the longest x6 15.5 us: spread_back(): column = column + jnp.roll(weighted * weights_z[off_z], off_z - 1, -1)]
  transfers between devices with their start and end apart: 32 -> 0, of which waited for: 19 -> 0; matrix products, arithmetic and copies ran while one was open for 1% -> 0% of each run, Pallas kernels for 0% -> 0%
where the time goes in v1:
time: 99.2 us; the launch traced here: 98.5 us
  Pallas kernels  94.5 us (95%)
  local copies, waits for them, and re-layouts  3.33 us (3%)
    pallas_call x1, Pallas kernels, on_device(): pl.pallas_call(make_kernel(count_x, count_y), name='adjoint', out_shape=(...  94.5 us
    unnamed x2, local copies, waits for them, and re-layouts  3.33 us

profile of v1, /device:TPU:0, one launch (start us, length us, event | category | flops | bytes accessed | tf_op | source)
XLA Modules:
  0.0 98.5 jit_solution(6287731852185303915)
XLA Ops:
  0.6 94.5 %adjoint.1 = (f32[16,16,128]{2,1,0:T(8,128)}, f32[3,16,16,128]{3,2,1,0:T(8,128)}) custom-call(f32[16,16,128]{2,1,0:T(8,128)} %lev.1, f32[3,16,16,128]{3,2,1,0:T(8,128)} %vel.1, s32[16,16,128]{2,1,0:T(8,128)} %lab.1, f32[2,3,16,16,128]{4,3,2,1,0:T(8,128)} %frac_any.1, s32[2]{0:T(128)} %bitcast.2, s32[2]{0:T(128)} %bitcast.3, f32[2]{0:T(128)} %rates.1), custom_call_target="tpu_custom_call" | custom-call | tf_op jit(solution)/shard_map/adjoint/pallas_call | solution.py:395
  95.1 1.6 %copy.11 = f32[16,16,128]{2,1,0:T(8,128)} copy(f32[16,16,128]{2,1,0:T(8,128)} %get-tuple-element.4) | data formatting | bytes 262144
  96.7 1.8 %copy.12 = f32[3,16,16,128]{3,2,1,0:T(8,128)} copy(f32[3,16,16,128]{3,2,1,0:T(8,128)} %get-tuple-element.5) | data formatting | bytes 786432

commit v2 on v1

--- a/solution.py
+++ b/solution.py
@@ -12,6 +12,14 @@
 ROW = (C, Z)
 HALO = 24
 PATCH = C + 3
+U_COEF, U_FIRST, U_SECOND, U_WEIGHT, U_SPREAD, U_BUILD = 3, 6, 4, 2, 2, 7
+ORDER = (
+    "d02", "s02", "d00", "s00", "g02", "d01", "s01", "g00", "s03", "c02", "c00", "g01",
+    "f02", "f00", "g03", "c01", "d12", "s12", "c03", "d10", "s10", "f01", "g12", "f03",
+    "s13", "g10", "c12", "d11", "s11", "c10", "g13", "f12", "g11", "c13", "f10", "c11",
+    "f13", "f11",
+)
+PARTS = 1
 
 PARTNERS = (
     [(d, 0) for d in (1, -1, 3, -3)]
@@ -36,15 +44,32 @@
     return value if shift == 0 else pltpu.roll(value, shift, axis)
 
 
+def loop(low, high, body, carry, width):
+    whole = (high - low) // width
+
+    def several(n, carry):
+        for k in range(width):
+            carry = body(low + n * width + k, carry)
+        return carry
+
+    if whole > 1:
+        carry = lax.fori_loop(0, whole, several, carry)
+    else:
+        whole = 0
+    for i in range(low + whole * width, high):
+        carry = body(i, carry)
+    return carry
+
+
 def make_kernel(count_x, count_y):
     def kernel(
-        lev, vel, lab, frac_any, sx, sy, rates,
+        lev_any, vel_any, lab_any, frac_any, sx, sy, rates,
         out_l, out_v,
-        frac, ext, mid, coef, dif, lvl, weight,
+        frac, lab, ext, mid, coef, dif, lvl, weight,
         to_up, to_down, to_rim, own, from_down, from_up, from_rim,
-        edge_r, edge_l, tail_r, tail_l, got_tail_r, got_tail_l,
-        got_r1, got_l1, next_r, next_l, got_r2, got_l2,
-        send_sem, recv_sem, frac_sem,
+        tail_r, tail_l, got_tail_r, got_tail_l,
+        far_r, far_l, near_r, near_l, got_far_r, got_far_l, got_near_r, got_near_l,
+        send_sem, recv_sem, load_sem,
     ):
         me_x = lax.axis_index("gx")
         me_y = lax.axis_index("gy")
@@ -52,12 +77,17 @@
         def partner(dx, dy):
             return (lax.rem(me_x + dx + count_x, count_x), lax.rem(me_y + dy + count_y, count_y))
 
-        frac_copy = pltpu.make_async_copy(frac_any, frac, frac_sem)
-        frac_copy.start()
-
         barrier = pltpu.get_barrier_semaphore()
         for dx, dy in PARTNERS:
             pl.semaphore_signal(barrier, inc=1, device_id=partner(dx, dy), device_id_type=MESH)
+
+        inner = ext.at[0, 0:3, 2 : C + 2, 0:C]
+        loads = [
+            pltpu.make_async_copy(src, dst, load_sem.at[n])
+            for n, (src, dst) in enumerate(((lab_any, lab), (vel_any, inner), (frac_any, frac), (lev_any, lvl)))
+        ]
+        for load in loads:
+            load.start()
 
         started = []
 
@@ -71,15 +101,15 @@
             started.append(copy)
             return copy
 
-        for f in range(3):
-            ext[0, f, 2 : C + 2, 0:C, :] = vel[f]
+        loads[0].wait()
         ext[0, 3, 2 : C + 2, 0:C, :] = jnp.where(lab[...] == 1, rates[1], rates[0])
+        loads[1].wait()
         pl.semaphore_wait(barrier, len(PARTNERS))
 
-        def send_halo(step, fields):
+        def send_halo(step, first, fields):
             e = ext.at[step]
             lo, hi = C, C + 2
-            f = pl.ds(0, fields)
+            f = pl.ds(first, fields)
             copies = [
                 send(e.at[f, lo:hi, 0:C], e.at[f, 0:2, 0:C], 1, 0),
                 send(e.at[f, 2:4, 0:C], e.at[f, hi : hi + 2, 0:C], -1, 0),
@@ -115,7 +145,7 @@
                     coef[n + 1, i] = k[n]
                 return carry
 
-            lax.fori_loop(1, C + 3, body, 0)
+            loop(1, C + 3, body, 0, U_COEF)
 
         def swept(src, f, i, height):
             v = src[f, i]
@@ -129,33 +159,31 @@
             total += coef[6, i, low] * rolled(v[low], 1, 1)
             return total
 
-        def diffuse(step):
+        def diffuse(step, f):
             def first(i, carry):
-                for f in range(3):
-                    mid[f, i] = swept(ext.at[step], f, i, HALO)
+                mid[f, i] = swept(ext.at[step], f, i, HALO)
                 return carry
 
-            lax.fori_loop(1, C + 3, first, 0)
+            loop(1, C + 3, first, 0, U_FIRST)
 
             def second(i, carry):
-                for f in range(3):
-                    dif[f, i - 2] = swept(mid, f, i, C)
+                dif[f, i - 2] = swept(mid, f, i, C)
                 return carry
 
-            lax.fori_loop(2, C + 2, second, 0)
+            loop(2, C + 2, second, 0, U_SECOND)
 
         def weights(step):
             def body(x, carry):
                 for n, value in enumerate(cubic_weights(frac[step, 2, x])):
-                    weight[n, x] = value
+                    weight[step, n, x] = value
                 for axis in range(2):
                     base = frac[step, axis, x]
                     for c in range(4):
                         for n, value in enumerate(cubic_weights(rolled(base, c - 1, 1))):
-                            weight[4 + 16 * axis + 4 * c + n, x] = value
+                            weight[step, 4 + 16 * axis + 4 * c + n, x] = value
                 return carry
 
-            lax.fori_loop(0, C, body, 0)
+            loop(0, C, body, 0, U_WEIGHT)
 
         line = lax.broadcasted_iota(jnp.int32, ROW, 0)
 
@@ -183,11 +211,11 @@
                     g = lvl[x] + BUOYANCY * dif[2, x]
                 sums = [[None] * 4 for _ in range(4)]
                 for c in range(4):
-                    gc = rolled(g * weight[c, x], c - 1, 1)
+                    gc = rolled(g * weight[step, c, x], c - 1, 1)
                     for b in range(4):
-                        h = gc * weight[20 + 4 * c + b, x]
+                        h = gc * weight[step, 20 + 4 * c + b, x]
                         for a in range(4):
-                            term = h * weight[4 + 4 * c + a, x]
+                            term = h * weight[step, 4 + 4 * c + a, x]
                             sums[a][b] = term if c == 0 else sums[a][b] + term
                 mains, rims = [], []
                 for a in range(4):
@@ -210,7 +238,14 @@
                 return (m1 + mains[1], m2 + mains[2], mains[3], r1 + rims[1], r2 + rims[2], rims[3])
 
             zero = jnp.zeros(ROW, jnp.float32)
-            m0, m1, m2, r0, r1, r2 = lax.fori_loop(0, C, body, (zero,) * 6)
+            half = C // 2
+            early, late = pl.ds(0, half), pl.ds(half, PATCH + 1 - half)
+            carry = loop(0, half, body, (zero,) * 6, U_SPREAD)
+            copies = [
+                send(to_up.at[slot, early], from_down.at[slot, early], 0, 1),
+                send(to_down.at[slot, early], from_up.at[slot, early], 0, -1),
+            ]
+            m0, m1, m2, r0, r1, r2 = loop(half, C, body, carry, U_SPREAD)
             emit(C, m0, r0)
             emit(C + 1, m1, r1)
             emit(C + 2, m2, r2)
@@ -219,9 +254,9 @@
             to_down[slot, PATCH] = meta
             to_rim[slot, PATCH] = meta
             own[slot, PATCH] = meta
-            return [
-                send(to_up.at[slot], from_down.at[slot], 0, 1),
-                send(to_down.at[slot], from_up.at[slot], 0, -1),
+            return copies + [
+                send(to_up.at[slot, late], from_down.at[slot, late], 0, 1),
+                send(to_down.at[slot, late], from_up.at[slot, late], 0, -1),
                 send(to_rim.at[slot, :, 0:2], from_rim.at[slot, :, 0:2], 0, 2),
                 send(to_rim.at[slot, :, C - 1 : C], from_rim.at[slot, :, C - 1 : C], 0, -2),
             ]
@@ -231,8 +266,9 @@
 
         def masks(slot, move):
             found = []
+            wanted = jnp.full(ROW, move, jnp.int32).astype(jnp.float32)
             for n, source in enumerate(sources):
-                hit = source[slot, PATCH] == float(move)
+                hit = source[slot, PATCH] == wanted
                 found.append(hit & rim_lines if n == 3 else hit)
             return found
 
@@ -243,64 +279,67 @@
                 total = part if total is None else total + part
             return total
 
-        def build(slot, move, store, load_extra=None):
+        def build(slot, move, low, high, store, load_extra=None):
             hits = masks(slot, move)
-            before = masks(slot, move - 1) if move > -2 else None
-            after = masks(slot, move + 1) if move < 2 else None
-
-            def row(q, extra_sum):
+
+            def row(q, rim):
                 total = gathered(slot, hits, q + 1)
                 if load_extra is not None:
                     total = total + load_extra(q)
-                if extra_sum is not None:
-                    total = total + extra_sum
+                if rim is not None:
+                    total = total + rim
                 store(q, total)
 
             def body(q, carry):
                 row(q, None)
                 return carry
 
-            first = 2 if before is not None else 0
-            last = C - 1 if after is not None else C
-            if before is not None:
+            first, last = low, high
+            if low == 0:
+                before = masks(slot, move - 1)
                 row(0, gathered(slot, before, C + 1))
                 row(1, gathered(slot, before, C + 2))
-            lax.fori_loop(first, last, body, 0)
-            if after is not None:
-                row(C - 1, gathered(slot, after, 0))
-
-        def store_to(ref, slot):
-            def store(q, value):
-                ref[slot, q] = value
-
-            return store
+                first = 2
+            if high == C:
+                last = C - 1
+            loop(first, last, body, 0, U_BUILD)
+            if high == C:
+                row(C - 1, gathered(slot, masks(slot, move + 1), 0))
+
+        def parts():
+            size = C // PARTS
+            return [(n * size, n * size + size) for n in range(PARTS)]
+
+        def transfer(slot, move, src, dst, dx, arrivals=None, arrived=None):
+            copies = []
+            for n, (low, high) in enumerate(parts()):
+                if arrivals is not None:
+                    arrivals[n].wait_recv()
+
+                def store(q, value):
+                    src[slot, q] = value
+
+                build(slot, move, low, high, store, None if arrived is None else lambda q: arrived[slot, q])
+                rows = pl.ds(low, high - low)
+                copies.append(send(src.at[slot, rows], dst.at[slot, rows], dx, 0))
+            return copies
 
         def outer(slot):
-            build(slot, 2, store_to(edge_r, slot))
-            copies = [send(edge_r.at[slot], got_r1.at[slot], 1, 0)]
-            build(slot, -2, store_to(edge_l, slot))
-            copies.append(send(edge_l.at[slot], got_l1.at[slot], -1, 0))
+            right = transfer(slot, 2, far_r, got_far_r, 1)
+            left = transfer(slot, -2, far_l, got_far_l, -1)
             hits = masks(slot, 2)
             tail_r[slot, 0] = gathered(slot, hits, C + 1)
             tail_r[slot, 1] = gathered(slot, hits, C + 2)
             tail_l[slot, 0] = gathered(slot, masks(slot, -2), 0)
-            copies.append(send(tail_r.at[slot], got_tail_r.at[slot], 3, 0))
-            copies.append(send(tail_l.at[slot], got_tail_l.at[slot], -3, 0))
-            return copies
-
-        def inner(slot, copies):
-            copies[0].wait_recv()
-            build(slot, 1, store_to(next_r, slot), lambda q: got_r1[slot, q])
-            right = send(next_r.at[slot], got_r2.at[slot], 1, 0)
-            copies[1].wait_recv()
-            build(slot, -1, store_to(next_l, slot), lambda q: got_l1[slot, q])
-            left = send(next_l.at[slot], got_l2.at[slot], -1, 0)
-            return [right, left, copies[2], copies[3]]
+            tails = [
+                send(tail_r.at[slot], got_tail_r.at[slot], 3, 0),
+                send(tail_l.at[slot], got_tail_l.at[slot], -3, 0),
+            ]
+            return right, left, tails
 
         def finish(slot, copies, load, store):
-            for copy in copies:
-                copy.wait_recv()
-            build(slot, 0, store, lambda q: got_r2[slot, q] + got_l2[slot, q])
+            wait_all(copies)
+            build(slot, 0, 0, C, store, lambda q: got_near_r[slot, q] + got_near_l[slot, q])
             store(0, load(0) + got_tail_r[slot, 0])
             store(1, load(1) + got_tail_r[slot, 1])
             store(C - 1, load(C - 1) + got_tail_l[slot, 0])
@@ -336,44 +375,42 @@
             for copy in copies:
                 copy.wait_recv()
 
-        halo = send_halo(0, 4)
-        lvl[...] = lev[...]
-        frac_copy.wait()
+        halo = {(0, f): [] for f in range(3)}
+        halo[0, 2] = send_halo(0, 0, 4)
+        loads[2].wait()
+        loads[3].wait()
         weights(1)
-        pending = None
-        for step in range(2):
-            when = 1 - step
-            base = 4 * step
-            wait_all(halo)
-            if step == 0:
+        weights(0)
+        state = {}
+
+        def do_d(step, f):
+            wait_all(halo[step, f])
+            if (step, f) == (0, 2):
                 coefficients()
-            diffuse(step)
-            chain = [None] * 4
-            passed = [None] * 4
-            passed[0] = spread(when, 0, base)
-            passed[1] = spread(when, 1, base + 1)
-            wait_all(passed[0])
-            chain[0] = outer(base)
-            passed[2] = spread(when, 2, base + 2)
-            wait_all(passed[1])
-            chain[1] = outer(base + 1)
-            if step == 1:
-                finish(base - 1, pending, *target(0, 3))
-            passed[3] = spread(when, 3, base + 3)
-            wait_all(passed[2])
-            chain[2] = outer(base + 2)
-            for f in range(3):
-                chain[f] = inner(base + f, chain[f])
-            wait_all(passed[3])
-            chain[3] = outer(base + 3)
-            if step == 0:
-                weights(0)
-            for f in range(3):
-                finish(base + f, chain[f], *target(step, f))
-            if step == 0:
-                halo = send_halo(1, 3)
-            pending = inner(base + 3, chain[3])
-        finish(7, pending, *target(1, 3))
+            diffuse(step, f)
+
+        def do_s(step, f):
+            state[step, f] = spread(1 - step, f, 4 * step + f)
+
+        def do_g(step, f):
+            wait_all(state[step, f])
+            state[step, f] = outer(4 * step + f)
+
+        def do_c(step, f):
+            right, left, rest = state[step, f]
+            slot = 4 * step + f
+            right = transfer(slot, 1, near_r, got_near_r, 1, right, got_far_r)
+            left = transfer(slot, -1, near_l, got_near_l, -1, left, got_far_l)
+            state[step, f] = right + left + rest
+
+        def do_f(step, f):
+            finish(4 * step + f, state[step, f], *target(step, f))
+            if step == 0 and f < 3:
+                halo[1, f] = send_halo(1, f, 1)
+
+        todo = {"d": do_d, "s": do_s, "g": do_g, "c": do_c, "f": do_f}
+        for word in ORDER:
+            todo[word[0]](int(word[1]), int(word[2]))
         for copy in started:
             copy.wait_send()
 
@@ -382,7 +419,7 @@
 
 def solution(mesh):
     count_x, count_y = mesh.shape["gx"], mesh.shape["gy"]
-    copies = 2 * (8 + 4 * 10)
+    copies = 8 + 3 * 8 + 2 * 4 * (6 + 2 + 4 * PARTS)
 
     def on_device(level, velocity, fraction, shift_x, shift_y, labels, rates):
         vmem = pl.BlockSpec(memory_space=pltpu.VMEM)
@@ -392,35 +429,51 @@
         def rows(*lead):
             return pltpu.VMEM(lead + ROW, f32)
 
-        return pl.pallas_call(
+        level_out, velocity_out = pl.pallas_call(
             make_kernel(count_x, count_y),
             name="adjoint",
             out_shape=(
                 jax.ShapeDtypeStruct((C, C, Z), f32),
                 jax.ShapeDtypeStruct((3, C, C, Z), f32),
             ),
-            in_specs=[vmem, vmem, vmem, pl.BlockSpec(memory_space=pl.ANY), smem, smem, smem],
+            in_specs=[pl.BlockSpec(memory_space=pl.ANY)] * 4 + [smem] * 3,
             out_specs=(vmem, vmem),
             scratch_shapes=[
                 rows(2, 3, C),
+                pltpu.VMEM((C, C, Z), jnp.int32),
                 pltpu.VMEM((2, 4, C + 4, HALO, Z), f32),
                 pltpu.VMEM((3, C + 4, HALO, Z), f32),
                 pltpu.VMEM((7, C + 4, HALO, Z), f32),
                 rows(3, C),
                 rows(C),
-                rows(36, C),
+                rows(2, 36, C),
                 rows(8, PATCH + 1), rows(8, PATCH + 1), rows(8, PATCH + 1), rows(8, PATCH + 1),
                 rows(8, PATCH + 1), rows(8, PATCH + 1), rows(8, PATCH + 1),
-                rows(8, C), rows(8, C), rows(8, 2), rows(8, 1), rows(8, 2), rows(8, 1),
-                rows(8, C), rows(8, C), rows(8, C), rows(8, C), rows(8, C), rows(8, C),
+                rows(8, 2), rows(8, 1), rows(8, 2), rows(8, 1),
+                rows(8, C), rows(8, C), rows(8, C), rows(8, C), rows(8, C), rows(8, C), rows(8, C), rows(8, C),
                 pltpu.SemaphoreType.DMA((copies,)),
                 pltpu.SemaphoreType.DMA((copies,)),
-                pltpu.SemaphoreType.DMA,
+                pltpu.SemaphoreType.DMA((4,)),
             ],
             compiler_params=pltpu.CompilerParams(
                 collective_id=0, has_side_effects=True, vmem_limit_bytes=56 * 2**20
             ),
         )(level, velocity, labels, fraction, shift_x.reshape(2), shift_y.reshape(2), rates)
+
+        def hand_over(a, b, to_a, to_b):
+            to_a[...] = a[...]
+            to_b[...] = b[...]
+
+        return pl.pallas_call(
+            hand_over,
+            name="hand_over",
+            out_shape=(
+                jax.ShapeDtypeStruct((C, C, Z), f32),
+                jax.ShapeDtypeStruct((3, C, C, Z), f32),
+            ),
+            in_specs=[vmem, vmem],
+            out_specs=(vmem, vmem),
+        )(level_out, velocity_out)
 
     field = P("gx", "gy", None)
     stack = P(None, "gx", "gy", None)

time: 99.2 us -> 80.7 us (0.81)
  Pallas kernels: 94.5 us -> 79.9 us
  local copies, waits for them, and re-layouts: 3.33 us -> 0 us
    pallas_call x1, Pallas kernels: 94.5 us -> 78 us  [on_device(): pl.pallas_call(make_kernel(count_x, count_y), name='adjoint', out_shape=(...]
    unnamed x2 -> x0, local copies, waits for them, and re-layouts: 3.33 us -> none
    pallas_call x0 -> x1, Pallas kernels: none -> 1.87 us  [on_device(): pl.pallas_call(hand_over, name='hand_over', out_shape=(jax.ShapeDtypeStru...]
where the time goes in v2:
time: 80.7 us; the launch traced here: 80.5 us
  Pallas kernels  79.9 us (99%)
    pallas_call x1, Pallas kernels, on_device(): pl.pallas_call(make_kernel(count_x, count_y), name='adjoint', out_shape=(...  78 us
    pallas_call x1, Pallas kernels, on_device(): pl.pallas_call(hand_over, name='hand_over', out_shape=(jax.ShapeDtypeStru...  1.87 us

profile of v2, /device:TPU:0, one launch (start us, length us, event | category | flops | bytes accessed | tf_op | source)
XLA Modules:
  0.0 80.5 jit_solution(4978088958483834603)
XLA Ops:
  0.6 78.0 %adjoint.1 = (f32[16,16,128]{2,1,0:T(8,128)}, f32[3,16,16,128]{3,2,1,0:T(8,128)}) custom-call(f32[16,16,128]{2,1,0:T(8,128)} %lev_any.1, f32[3,16,16,128]{3,2,1,0:T(8,128)} %vel_any.1, s32[16,16,128]{2,1,0:T(8,128)} %lab_any.1, f32[2,3,16,16,128]{4,3,2,1,0:T(8,128)} %frac_any.1, s32[2]{0:T(128)} %bitcast.2, s32[2]{0:T(128)} %bitcast.3, f32[2]{0:T(128)} %rates.1), custom_call_target="tpu_custom_call" | custom-call | tf_op jit(solution)/shard_map/adjoint/pallas_call | solution.py:432
  78.7 1.9 %hand_over.1 = (f32[16,16,128]{2,1,0:T(8,128)}, f32[3,16,16,128]{3,2,1,0:T(8,128)}) custom-call(f32[16,16,128]{2,1,0:T(8,128)} %get-tuple-element.4.a, f32[3,16,16,128]{3,2,1,0:T(8,128)} %get-tuple-element.5.b), custom_call_target="tpu_custom_call" | custom-call | tf_op jit(solution)/shard_map/hand_over/pallas_call | solution.py:467

commit v3 on v2

--- a/solution.py
+++ b/solution.py
@@ -14,17 +14,16 @@
 PATCH = C + 3
 U_COEF, U_FIRST, U_SECOND, U_WEIGHT, U_SPREAD, U_BUILD = 3, 6, 4, 2, 2, 7
 ORDER = (
-    "d02", "s02", "d00", "s00", "g02", "d01", "s01", "g00", "s03", "c02", "c00", "g01",
-    "f02", "f00", "g03", "c01", "d12", "s12", "c03", "d10", "s10", "f01", "g12", "f03",
-    "s13", "g10", "c12", "d11", "s11", "c10", "g13", "f12", "g11", "c13", "f10", "c11",
-    "f13", "f11",
+    "d02", "s02", "d00", "s00", "g02", "d01", "s01", "p02", "g00", "s03", "c02", "p00",
+    "c00", "g01", "p01", "f02", "f00", "g03", "c01", "d12", "s12", "p03", "c03", "d10",
+    "s10", "f01", "g12", "f03", "s13", "p12", "g10", "c12", "d11", "s11", "p10", "c10",
+    "g13", "f12", "g11", "p13", "c13", "f10", "p11", "c11", "f13", "f11",
 )
-PARTS = 1
 
 PARTNERS = (
-    [(d, 0) for d in (1, -1, 3, -3)]
-    + [(0, d) for d in (1, -1, 2, -2)]
-    + [(a, b) for a in (1, -1) for b in (1, -1)]
+    [(a, b) for a in (1, -1) for b in (1, -1)]
+    + [(d, 0) for d in (3, -3, 1, -1)]
+    + [(0, d) for d in (2, -2, 1, -1)]
 )
 
 
@@ -67,7 +66,7 @@
         out_l, out_v,
         frac, lab, ext, mid, coef, dif, lvl, weight,
         to_up, to_down, to_rim, own, from_down, from_up, from_rim,
-        tail_r, tail_l, got_tail_r, got_tail_l,
+        middle, tail_r, tail_l, got_tail_r, got_tail_l,
         far_r, far_l, near_r, near_l, got_far_r, got_far_l, got_near_r, got_near_l,
         send_sem, recv_sem, load_sem,
     ):
@@ -110,12 +109,7 @@
             e = ext.at[step]
             lo, hi = C, C + 2
             f = pl.ds(first, fields)
-            copies = [
-                send(e.at[f, lo:hi, 0:C], e.at[f, 0:2, 0:C], 1, 0),
-                send(e.at[f, 2:4, 0:C], e.at[f, hi : hi + 2, 0:C], -1, 0),
-                send(e.at[f, 2:hi, C - 2 : C], e.at[f, 2:hi, HALO - 2 : HALO], 0, 1),
-                send(e.at[f, 2:hi, 0:2], e.at[f, 2:hi, C : C + 2], 0, -1),
-            ]
+            copies = []
             for dx in (1, -1):
                 for dy in (1, -1):
                     src_i, dst_i = (hi - 1, 1) if dx == 1 else (2, hi)
@@ -127,6 +121,12 @@
                             dx, dy,
                         )
                     )
+            copies += [
+                send(e.at[f, lo:hi, 0:C], e.at[f, 0:2, 0:C], 1, 0),
+                send(e.at[f, 2:4, 0:C], e.at[f, hi : hi + 2, 0:C], -1, 0),
+                send(e.at[f, 2:hi, C - 2 : C], e.at[f, 2:hi, HALO - 2 : HALO], 0, 1),
+                send(e.at[f, 2:hi, 0:2], e.at[f, 2:hi, C : C + 2], 0, -1),
+            ]
             return copies
 
         def coefficients():
@@ -279,54 +279,33 @@
                 total = part if total is None else total + part
             return total
 
-        def build(slot, move, low, high, store, load_extra=None):
+        def build(slot, move, store):
             hits = masks(slot, move)
 
-            def row(q, rim):
-                total = gathered(slot, hits, q + 1)
-                if load_extra is not None:
-                    total = total + load_extra(q)
-                if rim is not None:
-                    total = total + rim
-                store(q, total)
-
             def body(q, carry):
-                row(q, None)
+                store(q, gathered(slot, hits, q + 1))
                 return carry
 
-            first, last = low, high
-            if low == 0:
+            first, last = 0, C
+            if move > -2:
                 before = masks(slot, move - 1)
-                row(0, gathered(slot, before, C + 1))
-                row(1, gathered(slot, before, C + 2))
+                for q in range(2):
+                    store(q, gathered(slot, hits, q + 1) + gathered(slot, before, C + 1 + q))
                 first = 2
-            if high == C:
+            if move < 2:
                 last = C - 1
             loop(first, last, body, 0, U_BUILD)
-            if high == C:
-                row(C - 1, gathered(slot, masks(slot, move + 1), 0))
-
-        def parts():
-            size = C // PARTS
-            return [(n * size, n * size + size) for n in range(PARTS)]
-
-        def transfer(slot, move, src, dst, dx, arrivals=None, arrived=None):
-            copies = []
-            for n, (low, high) in enumerate(parts()):
-                if arrivals is not None:
-                    arrivals[n].wait_recv()
-
-                def store(q, value):
-                    src[slot, q] = value
-
-                build(slot, move, low, high, store, None if arrived is None else lambda q: arrived[slot, q])
-                rows = pl.ds(low, high - low)
-                copies.append(send(src.at[slot, rows], dst.at[slot, rows], dx, 0))
-            return copies
+            if move < 2:
+                store(C - 1, gathered(slot, hits, C) + gathered(slot, masks(slot, move + 1), 0))
+
+        def transfer(slot, move, src, dst, dx):
+            def store(q, value):
+                src[slot, q] = value
+
+            build(slot, move, store)
+            return [send(src.at[slot], dst.at[slot], dx, 0)]
 
         def outer(slot):
-            right = transfer(slot, 2, far_r, got_far_r, 1)
-            left = transfer(slot, -2, far_l, got_far_l, -1)
             hits = masks(slot, 2)
             tail_r[slot, 0] = gathered(slot, hits, C + 1)
             tail_r[slot, 1] = gathered(slot, hits, C + 2)
@@ -335,41 +314,44 @@
                 send(tail_r.at[slot], got_tail_r.at[slot], 3, 0),
                 send(tail_l.at[slot], got_tail_l.at[slot], -3, 0),
             ]
+            right = transfer(slot, 2, far_r, got_far_r, 1)
+            left = transfer(slot, -2, far_l, got_far_l, -1)
             return right, left, tails
 
-        def finish(slot, copies, load, store):
+        def prepare(slot):
+            for move, ref in ((1, near_r), (-1, near_l), (0, middle)):
+                def store(q, value):
+                    ref[slot, q] = value
+
+                build(slot, move, store)
+
+        def pass_on(slot, near, got_far, got_near, dx, copies):
             wait_all(copies)
-            build(slot, 0, 0, C, store, lambda q: got_near_r[slot, q] + got_near_l[slot, q])
-            store(0, load(0) + got_tail_r[slot, 0])
-            store(1, load(1) + got_tail_r[slot, 1])
-            store(C - 1, load(C - 1) + got_tail_l[slot, 0])
+            near[slot] = near[slot] + got_far[slot]
+            return [send(near.at[slot], got_near.at[slot], dx, 0)]
+
+        def finish(slot, copies, store):
+            wait_all(copies)
+            for q in range(C):
+                total = middle[slot, q] + (got_near_r[slot, q] + got_near_l[slot, q])
+                if q < 2:
+                    total = total + got_tail_r[slot, q]
+                if q == C - 1:
+                    total = total + got_tail_l[slot, 0]
+                store(q, total)
 
         def target(step, f):
-            if step == 0 and f < 3:
-                def store(q, value):
+            def store(q, value):
+                if step == 0 and f < 3:
                     ext[1, f, q + 2, 0:C] = value
-
-                def load(q):
-                    return ext[1, f, q + 2, 0:C]
-            elif step == 0:
-                def store(q, value):
+                elif step == 0:
                     lvl[q] = value
-
-                def load(q):
-                    return lvl[q]
-            elif f < 3:
-                def store(q, value):
+                elif f < 3:
                     out_v[f, q] = value
-
-                def load(q):
-                    return out_v[f, q]
-            else:
-                def store(q, value):
+                else:
                     out_l[q] = value
 
-                def load(q):
-                    return out_l[q]
-            return load, store
+            return store
 
         def wait_all(copies):
             for copy in copies:
@@ -399,16 +381,19 @@
         def do_c(step, f):
             right, left, rest = state[step, f]
             slot = 4 * step + f
-            right = transfer(slot, 1, near_r, got_near_r, 1, right, got_far_r)
-            left = transfer(slot, -1, near_l, got_near_l, -1, left, got_far_l)
+            right = pass_on(slot, near_r, got_far_r, got_near_r, 1, right)
+            left = pass_on(slot, near_l, got_far_l, got_near_l, -1, left)
             state[step, f] = right + left + rest
 
+        def do_p(step, f):
+            prepare(4 * step + f)
+
         def do_f(step, f):
-            finish(4 * step + f, state[step, f], *target(step, f))
+            finish(4 * step + f, state[step, f], target(step, f))
             if step == 0 and f < 3:
                 halo[1, f] = send_halo(1, f, 1)
 
-        todo = {"d": do_d, "s": do_s, "g": do_g, "c": do_c, "f": do_f}
+        todo = {"d": do_d, "s": do_s, "g": do_g, "p": do_p, "c": do_c, "f": do_f}
         for word in ORDER:
             todo[word[0]](int(word[1]), int(word[2]))
         for copy in started:
@@ -419,7 +404,7 @@
 
 def solution(mesh):
     count_x, count_y = mesh.shape["gx"], mesh.shape["gy"]
-    copies = 8 + 3 * 8 + 2 * 4 * (6 + 2 + 4 * PARTS)
+    copies = 8 + 3 * 8 + 2 * 4 * 12
 
     def on_device(level, velocity, fraction, shift_x, shift_y, labels, rates):
         vmem = pl.BlockSpec(memory_space=pltpu.VMEM)
@@ -449,7 +434,7 @@
                 rows(2, 36, C),
                 rows(8, PATCH + 1), rows(8, PATCH + 1), rows(8, PATCH + 1), rows(8, PATCH + 1),
                 rows(8, PATCH + 1), rows(8, PATCH + 1), rows(8, PATCH + 1),
-                rows(8, 2), rows(8, 1), rows(8, 2), rows(8, 1),
+                rows(8, C), rows(8, 2), rows(8, 1), rows(8, 2), rows(8, 1),
                 rows(8, C), rows(8, C), rows(8, C), rows(8, C), rows(8, C), rows(8, C), rows(8, C), rows(8, C),
                 pltpu.SemaphoreType.DMA((copies,)),
                 pltpu.SemaphoreType.DMA((copies,)),

time: 80.7 us -> 80.4 us (level)
  no operation moved by 1% of the time
where the time goes in v3:
time: 80.4 us; the launch traced here: 80.2 us
  Pallas kernels  79.6 us (99%)
    pallas_call x1, Pallas kernels, on_device(): pl.pallas_call(make_kernel(count_x, count_y), name='adjoint', out_shape=(...  77.7 us
    pallas_call x1, Pallas kernels, on_device(): pl.pallas_call(hand_over, name='hand_over', out_shape=(jax.ShapeDtypeStru...  1.87 us

profile of v3, /device:TPU:0, one launch (start us, length us, event | category | flops | bytes accessed | tf_op | source)
XLA Modules:
  0.0 80.2 jit_solution(4159153844275782305)
XLA Ops:
  0.6 77.7 %adjoint.1 = (f32[16,16,128]{2,1,0:T(8,128)}, f32[3,16,16,128]{3,2,1,0:T(8,128)}) custom-call(f32[16,16,128]{2,1,0:T(8,128)} %lev_any.1, f32[3,16,16,128]{3,2,1,0:T(8,128)} %vel_any.1, s32[16,16,128]{2,1,0:T(8,128)} %lab_any.1, f32[2,3,16,16,128]{4,3,2,1,0:T(8,128)} %frac_any.1, s32[2]{0:T(128)} %bitcast.2, s32[2]{0:T(128)} %bitcast.3, f32[2]{0:T(128)} %rates.1), custom_call_target="tpu_custom_call" | custom-call | tf_op jit(solution)/shard_map/adjoint/pallas_call | solution.py:417
  78.4 1.9 %hand_over.1 = (f32[16,16,128]{2,1,0:T(8,128)}, f32[3,16,16,128]{3,2,1,0:T(8,128)}) custom-call(f32[16,16,128]{2,1,0:T(8,128)} %get-tuple-element.4.a, f32[3,16,16,128]{3,2,1,0:T(8,128)} %get-tuple-element.5.b), custom_call_target="tpu_custom_call" | custom-call | tf_op jit(solution)/shard_map/hand_over/pallas_call | solution.py:452
